TPU v7x, 256 devices: a whole 4x4x8 slice. The times are simulated.
256 devices in a mesh: pool: 2 (over core), group: 32 (over x, y, z_hi), tensor: 4 (over z_lo).
Axes of the slice: x: 4, y: 4, z: 8 (z_hi: 2, z_lo: 4; z = z_hi * 4 + z_lo), core: 2. Of those that a mesh axis runs over, the one named last changes fastest.
Arguments:
- queries: bfloat16 [2, 6144, 5120], P('pool', 'group', 'tensor'), may hold values from -8 to 8
- new_keys: bfloat16 [2, 6144, 1024], P('pool', 'group', 'tensor'), may hold values from -8 to 8
- new_values: bfloat16 [2, 6144, 1024], P('pool', 'group', 'tensor'), may hold values from -6 to 6
- cache_keys: bfloat16 [2, 32, 4096, 1024], P('pool', 'group', None, 'tensor'), may hold values from -8 to 8
- cache_values: bfloat16 [2, 32, 4096, 1024], P('pool', 'group', None, 'tensor'), may hold values from -6 to 6
- prefix_len: int32 [2, 32], P('pool', 'group'), may hold values from 1 to 4096, as said below
- span_len: int32 [2, 32], P('pool', 'group'), may hold values from 1 to 192, as said below
- residual: bfloat16 [2, 6144, 5120], P('pool', 'group', 'tensor'), may hold values from -60 to 60
- out_proj: bfloat16 [2, 5120, 5120], P('pool', 'tensor', 'group'), may hold values from -1.1953125 to 1.1953125
- norm_gain: float32 [2, 5120], P('pool', 'tensor'), may hold values from 0.5 to 1.5
Outputs:
- stream: bfloat16 [2, 6144, 5120], P('pool', 'group', 'tensor')
- normed: bfloat16 [2, 6144, 5120], P('pool', 'group', 'tensor')
Inputs may be any that keep to these rules, and one draw needn't show every extreme that they name: `prefix_len`: in each pool some sequence has exactly 4096 cached tokens. `span_len`: most spans are full; in each pool some span has 192 real tokens.
All inputs are finite; a program needn't handle non-finite values.
Results may differ from a plain program's by a relative error of at most 0.0055.
Values may be sent and summed in bfloat16 or wider, within the bound.
A program may use at most 128 MiB of HBM per device.

v0:
```python
import functools
import math

import jax
import jax.numpy as jnp
from jax import lax
from jax.experimental import pallas as pl
from jax.experimental.pallas import tpu as pltpu
from jax.sharding import PartitionSpec as P

D = 5120
HD = 128
KVL = 2
GROUP_HEADS = 5
PREFIX = 4096
SPAN = 192
ROWS = GROUP_HEADS * SPAN
HALF = GROUP_HEADS * HD
EPSILON = 1e-6
KEY_BLOCK = 2048
BLOCKS = PREFIX // KEY_BLOCK
PIECE = 320
WCOLS = 160
WHALF = 80
LOG2 = math.log2(math.e) / math.sqrt(HD)
MASKED = -1e30
MESH = pl.DeviceIdType.MESH


def nt(a, b, precision=None):
    return lax.dot_general(
        a, b, (((1,), (1,)), ((), ())), preferred_element_type=jnp.float32, precision=precision
    )


def body(
    plen_ref, slen_ref, q_hbm, k_hbm, v_hbm, sk_hbm, sv_hbm, res_hbm, w_hbm, gain_ref,
    stream_hbm, normed_hbm,
    q_ref, k_ref, v_ref, sk_ref, sv_ref, res_ref, p32, rp, tiles,
    qs, S, Sp, mx, acc, va, vas,
    wg, ag, pr, pb, rcv1, s2, rcv2, rres, rt, turn, lb, st, mid, sums, mean, means,
    in_sem, w_loc, w_zs, w_xs, w_rs, a_ss, a_rs, res_ss, res_rs,
    p1_ss, p1_rs, p2_ss, p2_rs, f_ss, f_rs, g_ss, g_rs, q_ss, q_rs, m_ss, m_rs, out_sem,
):
    pool = lax.axis_index("pool")
    group = lax.axis_index("group")
    t = lax.axis_index("tensor")
    h = lax.rem(group, 2)
    y = lax.rem(lax.div(group, 2), 4)
    x = lax.div(group, 8)
    ylo = lax.rem(y, 2)
    yhi = lax.div(y, 2)
    zero_pool = pool == 0

    def device(px, xx, yy, hh, tt):
        return (px, (xx * 4 + yy) * 2 + hh, tt)

    def remote(src, dst, send, recv, where):
        return pltpu.make_async_remote_copy(
            src_ref=src, dst_ref=dst, send_sem=send, recv_sem=recv, device_id=where,
            device_id_type=MESH,
        )

    barrier = pltpu.get_barrier_semaphore()
    peers = [
        (lax.rem(y + k // 4, 4), lax.rem(t + k % 4, 4)) for k in range(1, 16)
    ]
    friends = [device(pool, x, yy, h, tt) for yy, tt in peers]
    friends += [device(pool, x, a, 1 - h, t) for a in range(4)]
    friends += [device(pool, lax.rem(x + k, 4), y, h, t) for k in (1, 2, 3)]
    friends += [device(1 - pool, x, a, b, t) for a in range(4) for b in range(2)]
    for friend in friends:
        pl.semaphore_signal(barrier, 1, device_id=friend, device_id_type=MESH)

    def put(s, rows, value):
        blank = jnp.zeros((value.shape[0], 3 * HD - PIECE), jnp.float32)
        full = jnp.concatenate([value, blank], axis=1)
        for c in range(3):
            p32[s, c, rows, :] = full[:, c * HD : (c + 1) * HD]

    def get(s, rows):
        full = jnp.concatenate([p32[s, c, rows, :] for c in range(3)], axis=1)
        return full[:, :PIECE]

    every = slice(0, SPAN)

    def every_fourth(k):
        return pl.ds(k, SPAN // 4, stride=4)


    def load(src, dst, index):
        copy = pltpu.make_async_copy(src, dst, in_sem.at[index])
        copy.start()
        return copy

    load_q = load(q_hbm, q_ref, 0)
    load_sk = load(sk_hbm, sk_ref, 1)
    load_sv = load(sv_hbm, sv_ref, 2)
    load_k = [
        load(k_hbm.at[pl.ds(j * KEY_BLOCK, KEY_BLOCK)], k_ref.at[pl.ds(j * KEY_BLOCK, KEY_BLOCK)], 3 + j)
        for j in range(BLOCKS)
    ]
    load_v = load(v_hbm, v_ref, 3 + BLOCKS)
    load_res = load(res_hbm, res_ref, 4 + BLOCKS)

    sums[y * 4 + t] = jnp.zeros((8, 2 * SPAN), jnp.float32)

    def w_half(hh, xx, part):
        return wg.at[hh, pl.ds(pl.multiple_of(xx * WCOLS + part * WHALF, 16), WHALF)]

    def w_from(part):
        return w_hbm.at[pl.ds(part * WHALF, WHALF)]

    z_partner = device(pool, x, y, 1 - h, t)
    x_up, x_down, x_far = lax.rem(x + 1, 4), lax.rem(x + 3, 4), lax.rem(x + 2, 4)
    own_w = pltpu.make_async_copy(
        w_hbm, wg.at[h, pl.ds(pl.multiple_of(x * WCOLS, WCOLS), WCOLS)], w_loc
    )
    own_w.start()
    w_over = [
        remote(w_from(part), w_half(h, x, part), w_zs.at[part], w_rs.at[h, x, part], z_partner)
        for part in range(2)
    ]

    def w_send(source, hh, xx, part, wave, way, to_x):
        return remote(
            source, w_half(hh, xx, part), w_xs.at[wave, part, way], w_rs.at[hh, xx, part],
            device(pool, to_x, y, h, t),
        )

    def w_direct(wave):
        hh = h if wave == 0 else 1 - h
        out = []
        for part in range(2):
            source = w_from(part) if wave == 0 else w_half(hh, x, part)
            ways = [(0, x_up), (1, x_down)]
            for way, to_x in ways if part == 0 else ways[::-1]:
                out.append(w_send(source, hh, x, part, wave, way, to_x))
        return out

    def w_onward(wave):
        hh = h if wave == 0 else 1 - h
        return [
            w_send(w_half(hh, x_down, 0), hh, x_down, 0, wave, 2, x_up),
            w_send(w_half(hh, x_up, 1), hh, x_up, 1, wave, 2, x_down),
        ]

    def w_wait(hh, xx, part):
        remote(
            w_half(hh, xx, part), w_half(hh, xx, part), w_zs.at[0], w_rs.at[hh, xx, part], z_partner
        ).wait_recv()

    def pass_on(wave):
        hh = h if wave == 0 else 1 - h
        copies = w_onward(wave)
        w_wait(hh, x_down, 0)
        copies[0].start()
        w_wait(hh, x_up, 1)
        copies[1].start()
        return copies

    def w_rest(hh):
        w_wait(hh, x_down, 1)
        w_wait(hh, x_up, 0)
        w_wait(hh, x_far, 0)
        w_wait(hh, x_far, 1)

    def res_plan(s):
        to_y = jnp.where(zero_pool, ylo * 2 + h, s)
        to_h = jnp.where(zero_pool, s % 2, h)
        slot = jnp.where(zero_pool, yhi * 2 + s // 2, y)
        keeps = jnp.logical_and(to_y == y, to_h == h)
        return keeps, slot, device(pool, x, to_y, to_h, t)

    def res_copies(s):
        keeps, slot, where = res_plan(s)
        near = pltpu.make_async_copy(rp.at[s], rres.at[slot], res_rs.at[slot])
        far = remote(rp.at[s], rres.at[slot], res_ss.at[s], res_rs.at[slot], where)
        return keeps, near, far

    plen = plen_ref[0, 0]
    slen = slen_ref[0, 0]
    row_at = lax.broadcasted_iota(jnp.int32, (SPAN, SPAN), 0)
    col_at = lax.broadcasted_iota(jnp.int32, (SPAN, SPAN), 1)
    span_mask = (col_at <= row_at) & (col_at < slen)

    def head_rows(g):
        return slice(g * SPAN, (g + 1) * SPAN)

    def head_cols(hd, g):
        return slice((hd * GROUP_HEADS + g) * HD, (hd * GROUP_HEADS + g + 1) * HD)

    def span_scores(hd):
        for g in range(GROUP_HEADS):
            s = nt(qs[hd, head_rows(g), :], sk_ref[:, hd * HD : (hd + 1) * HD])
            s = jnp.where(span_mask, s, MASKED)
            Sp[hd, head_rows(g), :] = s
            rest = s[:, HD:]
            mx[hd, head_rows(g), :] = jnp.maximum(
                s[:, :HD], jnp.concatenate([rest, rest], axis=1)
            )

    def scores(hd, j):
        base = pl.multiple_of(j * KEY_BLOCK, KEY_BLOCK)
        keys = k_ref[pl.ds(base, KEY_BLOCK), hd * HD : (hd + 1) * HD]
        position = base + lax.broadcasted_iota(jnp.int32, (1, KEY_BLOCK), 1)
        bias = jnp.where(position < plen, 0.0, MASKED)
        slot = lax.rem(hd * BLOCKS + j, 3)
        for g in range(GROUP_HEADS):
            s = nt(qs[hd, head_rows(g), :], keys) + bias
            S[slot, head_rows(g), :] = s
            m = mx[hd, head_rows(g), :]
            for u in range(0, KEY_BLOCK, HD):
                m = jnp.maximum(m, s[:, u : u + HD])
            mx[hd, head_rows(g), :] = m

    def finish_max(hd):
        m = jnp.max(mx[hd], axis=1, keepdims=True) * LOG2
        mx[hd] = jnp.broadcast_to(m, (ROWS, HD))

    def weigh(hd, j):
        base = pl.multiple_of(j * KEY_BLOCK, KEY_BLOCK)
        values = va[hd, pl.ds(base, KEY_BLOCK), :]
        slot = lax.rem(hd * BLOCKS + j, 3)
        for g in range(GROUP_HEADS):
            m = mx[hd, head_rows(g), :]
            wide = jnp.concatenate([m] * (KEY_BLOCK // HD), axis=1)
            p = jnp.exp2(S[slot, head_rows(g), :] * LOG2 - wide).astype(jnp.bfloat16)
            acc[hd, head_rows(g), :] += jnp.dot(p, values, preferred_element_type=jnp.float32)

    def span_weigh(hd):
        for g in range(GROUP_HEADS):
            m = mx[hd, head_rows(g), :]
            wide = jnp.concatenate([m, m[:, : SPAN - HD]], axis=1)
            p = jnp.exp2(Sp[hd, head_rows(g), :] * LOG2 - wide).astype(jnp.bfloat16)
            acc[hd, head_rows(g), :] = jnp.dot(p, vas[hd], preferred_element_type=jnp.float32)

    def a_slot(hd, yy):
        return ag.at[hd, pl.ds(pl.multiple_of(yy * SPAN, SPAN), SPAN)]

    def attended(hd):
        for g in range(GROUP_HEADS):
            a = acc[hd, head_rows(g), :]
            out = (a[:, :HD] / a[:, HD:]).astype(jnp.bfloat16)
            ag[hd, pl.ds(pl.multiple_of(y * SPAN, SPAN), SPAN), g * HD : (g + 1) * HD] = out

    y_partners = [yhi * 2 + 1 - ylo, (1 - yhi) * 2 + ylo, (1 - yhi) * 2 + 1 - ylo]

    y_up, y_down = lax.rem(y + 1, 4), lax.rem(y + 3, 4)

    def a_copy(hd, yy, i, to_y):
        return remote(a_slot(hd, yy), a_slot(hd, yy), a_ss.at[hd, i], a_rs.at[hd, yy], device(pool, x, to_y, h, t))

    def a_copies(hd):
        return [a_copy(hd, y, 0, y_up), a_copy(hd, y, 1, y_down)]

    def a_arrival(hd, yy):
        return remote(a_slot(hd, yy), a_slot(hd, yy), a_ss.at[hd, 0], a_rs.at[hd, yy], z_partner)

    pl.semaphore_wait(barrier, len(friends))
    w_first = w_direct(0)
    for copy in w_over + w_first:
        copy.start()
    load_q.wait()
    for hd in range(KVL):
        for g in range(GROUP_HEADS):
            qs[hd, head_rows(g), :] = q_ref[:, head_cols(hd, g)]
    load_sk.wait()
    span_scores(0)
    for copy in load_k:
        copy.wait()
    pl.loop(0, BLOCKS)(lambda j: scores(0, j))
    load_v.wait()
    load_sv.wait()
    for hd in range(KVL):
        va[hd, :, :HD] = v_ref[:, hd * HD : (hd + 1) * HD]
        va[hd, :, HD:] = jnp.ones((PREFIX, HD), jnp.bfloat16)
        vas[hd, :, :HD] = sv_ref[:, hd * HD : (hd + 1) * HD]
        vas[hd, :, HD:] = jnp.ones((SPAN, HD), jnp.bfloat16)
    finish_max(0)
    span_weigh(0)
    span_scores(1)

    def middle(j):
        weigh(0, j)
        scores(1, j)

    pl.loop(0, BLOCKS)(middle)
    attended(0)
    first_a = a_copies(0)
    for copy in first_a:
        copy.start()
    w_first += pass_on(0)
    finish_max(1)
    span_weigh(1)
    pl.loop(0, BLOCKS)(lambda j: weigh(1, j))
    attended(1)
    second_a = a_copies(1)
    for copy in second_a:
        copy.start()

    w_second = w_direct(1)
    for part in range(2):
        w_wait(1 - h, x, part)
        for copy in w_second[2 * part : 2 * part + 2]:
            copy.start()
    a_arrival(1, y_up).wait_recv()
    pass_second = a_copy(1, y_up, 2, y_down)
    pass_second.start()
    a_arrival(0, y_down).wait_recv()
    pass_first = a_copy(0, y_down, 2, y_up)
    pass_first.start()

    load_res.wait()

    @pl.when(zero_pool)
    def _():
        for s in range(4):
            rows = res_ref[s * (SPAN // 4) : (s + 1) * (SPAN // 4), :].astype(jnp.float32)
            for k in range(4):
                put(s, every_fourth(k), rows[:, k * PIECE : (k + 1) * PIECE])

    @pl.when(jnp.logical_not(zero_pool))
    def _():
        for s in range(4):
            put(s, every, res_ref[:, s * PIECE : (s + 1) * PIECE].astype(jnp.float32))

    for s in range(4):
        rp[s] = get(s, every).astype(jnp.bfloat16)
        keeps, near, far = res_copies(s)

        @pl.when(keeps)
        def _():
            near.start()

        @pl.when(jnp.logical_not(keeps))
        def _():
            far.start()

    t1 = t + 1 - 2 * lax.rem(t, 2)
    t2 = lax.rem(t + 2, 4)
    t3 = 3 - t
    tpar = lax.rem(t, 2)
    thi = lax.div(t, 2)

    def piece_rows(piece):
        return pl.ds(pl.multiple_of(piece * WCOLS, WCOLS), WCOLS)

    def p1_copy(u, i, piece):
        return remote(
            pb.at[u, piece_rows(piece)], rcv1.at[lax.div(piece, 2), u], p1_ss.at[u, i],
            p1_rs.at[lax.div(piece, 2), u], device(pool, x, y, h, t1),
        )

    def p1_arrival(jj, u):
        return remote(rcv1.at[jj, u], rcv1.at[jj, u], p1_ss.at[u, 0], p1_rs.at[jj, u], z_partner)

    def p2_copy(u):
        return remote(s2.at[u], rcv2.at[u], p2_ss.at[u], p2_rs.at[u], device(pool, x, y, h, t2))

    def unit(u):
        hh = h if u < 2 else 1 - h
        pair = yhi if u % 2 == 0 else 1 - yhi
        rows = pl.ds(pl.multiple_of(pair * 2 * SPAN, 2 * SPAN), 2 * SPAN)
        total = nt(wg[hh, :, :HALF], ag[0, rows, :]) + nt(wg[hh, :, HALF:], ag[1, rows, :])
        pr[u] = total
        pb[u] = total.astype(jnp.bfloat16)
        copy = p1_copy(u, 0, t3)
        copy.start()
        return copy

    def last_part(u):
        copy = p1_copy(u, 1, t1)
        copy.start()
        return copy

    def second(u):
        p1_arrival(1 - thi, u).wait_recv()
        total = pr[u, piece_rows(t2), :] + rcv1[1 - thi, u].astype(jnp.float32)
        s2[u] = total.astype(jnp.bfloat16)
        copy = p2_copy(u)
        copy.start()
        return copy

    p1_sent = []
    p2_sent = []
    own_w.wait()
    w_rest(h)
    first_head = jnp.where(ylo == 0, 0, 1)
    a_arrival(first_head, y_partners[0]).wait_recv()
    p1_sent.append(unit(0))
    p1_sent.append(last_part(0))
    w_second += pass_on(1)
    a_arrival(1 - first_head, y_partners[2]).wait_recv()
    for hd in range(KVL):
        a_arrival(hd, y_partners[1]).wait_recv()
    p1_sent.append(unit(1))
    p2_sent.append(second(0))
    p1_sent.append(last_part(1))
    p2_sent.append(second(1))

    for pair in range(2):
        for a in range(2):
            at = pair * 2 + a
            pltpu.make_async_copy(rres.at[at], rres.at[at], res_rs.at[at]).wait()
        both = jnp.concatenate([rres[pair * 2], rres[pair * 2 + 1]], axis=0).astype(jnp.float32)
        blank = jnp.zeros((2 * SPAN, 3 * HD - PIECE), jnp.float32)
        rt[pair] = jnp.transpose(jnp.concatenate([both, blank], axis=1))

    w_rest(1 - h)
    p1_sent.append(unit(2))
    p1_sent.append(unit(3))
    p2_sent.append(second(2))
    p1_sent.append(last_part(2))
    p2_sent.append(second(3))
    p1_sent.append(last_part(3))

    def final_copy(s, slot_from, index):
        to_y = jnp.where(zero_pool, s, lax.div(s, 2) * 2 + yhi)
        to_h = jnp.where(zero_pool, h, ylo)
        slot = jnp.where(zero_pool, y, lax.rem(s, 2) * 2 + h)
        return remote(
            lb.at[slot_from], st.at[slot], f_ss.at[index], f_rs.at[slot],
            device(1 - pool, x, to_y, to_h, t),
        )

    def detour(s, slot_from, index):
        to_y = lax.div(s, 2) * 2 + yhi
        crosses = jnp.logical_and(jnp.logical_not(zero_pool), h != ylo)
        part = lax.rem(s, 2)
        copy = remote(
            lb.at[slot_from], mid.at[part], f_ss.at[index], g_rs.at[part],
            device(pool, x, to_y, h, t),
        )
        return jnp.logical_and(crosses, to_y != y), copy

    carries = jnp.logical_and(jnp.logical_not(zero_pool), ylo * 2 + 1 - h != y)

    def carried(a):
        return remote(
            mid.at[a], st.at[a * 2 + h], g_ss.at[a], f_rs.at[a * 2 + h],
            device(1 - pool, x, y, 1 - h, t),
        )

    turn[pl.ds(PIECE, 64), :] = jnp.zeros((64, 2 * SPAN), jnp.float32)
    own_index = y * 4 + t
    final_sent = []
    sum_sent = []
    for pp in range(2):
        pair = yhi if pp == 0 else 1 - yhi
        squares = jnp.zeros((1, 2 * SPAN), jnp.float32)
        for hh in range(2):
            u = hh * 2 + pp
            at = h if hh == 0 else 1 - h
            p1_arrival(thi, u).wait_recv()
            p2_copy(u).wait_recv()
            rows = pl.ds(pl.multiple_of(at * WCOLS, WCOLS), WCOLS)
            total = (
                pr[u, piece_rows(t), :]
                + rcv1[thi, u].astype(jnp.float32)
                + rcv2[u].astype(jnp.float32)
                + rt[pair, rows, :]
            )
            total = total.astype(jnp.bfloat16).astype(jnp.float32)
            turn[rows, :] = total
            squares = squares + jnp.sum(total * total, axis=0, keepdims=True)
        sums[own_index, pl.ds(pair, 1), :] = squares
        if pp == 1:
            for k, (yy, tt) in enumerate(peers):
                copy = remote(
                    sums.at[own_index], sums.at[own_index], q_ss.at[k], q_rs.at[own_index],
                    device(pool, x, yy, h, tt),
                )
                copy.start()
                sum_sent.append(copy)
        whole = jnp.transpose(turn[...])[:, :PIECE].astype(jnp.bfloat16)
        for a in range(2):
            lb[pp * 2 + a] = whole[a * SPAN : (a + 1) * SPAN]
            copy = final_copy(pair * 2 + a, pp * 2 + a, pp * 2 + a)
            hops, around = detour(pair * 2 + a, pp * 2 + a, pp * 2 + a)

            @pl.when(hops)
            def _():
                around.start()

            @pl.when(jnp.logical_not(hops))
            def _():
                copy.start()

            final_sent.append(copy)

    @pl.when(carries)
    def _():
        for a in range(2):
            remote(mid.at[a], mid.at[a], g_ss.at[a], g_rs.at[a], z_partner).wait_recv()
            carried(a).start()

    total = sums[own_index]
    for k, (yy, tt) in enumerate(peers):
        index = yy * 4 + tt
        remote(sums.at[index], sums.at[index], q_ss.at[k], q_rs.at[index], z_partner).wait_recv()
        total = total + sums[index]
    mean[...] = total * (1.0 / D)
    for b in range(2):
        copy = remote(mean, means.at[h], m_ss.at[b], m_rs.at[h], device(1 - pool, x, y, b, t))
        copy.start()
        sum_sent.append(copy)

    for s in range(4):
        remote(lb.at[s], st.at[s], f_ss.at[s], f_rs.at[s], z_partner).wait_recv()
        put(s, every, st[s].astype(jnp.float32))

    def lay_out(at):
        @pl.when(zero_pool)
        def _():
            for s in range(4):
                quarter = [get(s, every_fourth(k)) for k in range(4)]
                tiles[at, s * (SPAN // 4) : (s + 1) * (SPAN // 4), :] = jnp.concatenate(
                    quarter, axis=1
                ).astype(jnp.bfloat16)

        @pl.when(jnp.logical_not(zero_pool))
        def _():
            tiles[at] = jnp.concatenate([get(s, every) for s in range(4)], axis=1).astype(jnp.bfloat16)

    lay_out(0)
    stream_out = pltpu.make_async_copy(tiles.at[0], stream_hbm.at[0], out_sem.at[0])
    stream_out.start()
    gains = [gain_ref[:, r * PIECE : (r + 1) * PIECE] for r in range(4)]

    def gain_at(s):
        return jnp.where(zero_pool, ylo * 2 + h, s)

    blank = jnp.zeros((1, 3 * HD - PIECE), jnp.float32)
    sub = lax.broadcasted_iota(jnp.int32, (8, 2 * SPAN), 0)
    scales = []
    for b in range(2):
        remote(mean, means.at[b], m_ss.at[b], m_rs.at[b], z_partner).wait_recv()
        scales.append(lax.rsqrt(means[b] + EPSILON))
    for s in range(4):
        from_h = jnp.where(zero_pool, s % 2, h)
        from_a = jnp.where(zero_pool, s // 2, ylo)
        picked = jnp.where(from_h == 0, scales[0], scales[1])
        row = jnp.sum(jnp.where(sub == yhi, picked, 0.0), axis=0, keepdims=True)
        row = jnp.where(from_a == 0, row[:, : 2 * HD], row[:, 2 * SPAN - 2 * HD :])
        turned = jnp.transpose(jnp.broadcast_to(row, (HD, 2 * HD)))
        wide = jnp.where(from_a == 0, turned[:SPAN], turned[2 * HD - SPAN :])
        gain = gains[0]
        for r in range(4):
            gain = jnp.where(gain_at(s) == r, gains[r], gain)
        gain = jnp.concatenate([gain, blank], axis=1)
        for c in range(3):
            p32[s, c] = p32[s, c] * wide * gain[:, c * HD : (c + 1) * HD]
    lay_out(1)
    normed_out = pltpu.make_async_copy(tiles.at[1], normed_hbm.at[0], out_sem.at[1])
    normed_out.start()

    @pl.when(carries)
    def _():
        for a in range(2):
            carried(a).wait_send()

    for copy in w_over + [pass_first, pass_second] + w_first + w_second + first_a + second_a + p1_sent + p2_sent + final_sent + sum_sent:
        copy.wait_send()
    for s in range(4):
        keeps, near, far = res_copies(s)

        @pl.when(jnp.logical_not(keeps))
        def _():
            far.wait_send()

    stream_out.wait()
    normed_out.wait()


def fused(plen, slen, q, k, v, sk, sv, res, w, gain):
    smem = pl.BlockSpec(memory_space=pltpu.SMEM)
    vmem = pl.BlockSpec(memory_space=pltpu.VMEM)
    hbm = pl.BlockSpec(memory_space=pl.ANY)
    dma = pltpu.SemaphoreType.DMA
    bf, f32 = jnp.bfloat16, jnp.float32
    out = jax.ShapeDtypeStruct((1, SPAN, 2 * HALF), bf)
    return pl.pallas_call(
        body,
        out_shape=(out, out),
        in_specs=[smem, smem] + [hbm] * 7 + [vmem],
        out_specs=(hbm, hbm),
        scratch_shapes=[
            pltpu.VMEM((SPAN, 2 * HALF), bf),
            pltpu.VMEM((PREFIX, KVL * HD), bf),
            pltpu.VMEM((PREFIX, KVL * HD), bf),
            pltpu.VMEM((SPAN, KVL * HD), bf),
            pltpu.VMEM((SPAN, KVL * HD), bf),
            pltpu.VMEM((SPAN, 2 * HALF), bf),
            pltpu.VMEM((4, 3, SPAN, HD), f32),
            pltpu.VMEM((4, SPAN, PIECE), bf),
            pltpu.VMEM((2, SPAN, 2 * HALF), bf),
            pltpu.VMEM((KVL, ROWS, HD), bf),
            pltpu.VMEM((3, ROWS, KEY_BLOCK), f32),
            pltpu.VMEM((KVL, ROWS, SPAN), f32),
            pltpu.VMEM((KVL, ROWS, HD), f32),
            pltpu.VMEM((KVL, ROWS, 2 * HD), f32),
            pltpu.VMEM((KVL, PREFIX, 2 * HD), bf),
            pltpu.VMEM((KVL, SPAN, 2 * HD), bf),
            pltpu.VMEM((2, 4 * WCOLS, 2 * HALF), bf),
            pltpu.VMEM((KVL, 4 * SPAN, HALF), bf),
            pltpu.VMEM((4, 4 * WCOLS, 2 * SPAN), f32),
            pltpu.VMEM((4, 4 * WCOLS, 2 * SPAN), bf),
            pltpu.VMEM((2, 4, WCOLS, 2 * SPAN), bf),
            pltpu.VMEM((4, WCOLS, 2 * SPAN), bf),
            pltpu.VMEM((4, WCOLS, 2 * SPAN), bf),
            pltpu.VMEM((4, SPAN, PIECE), bf),
            pltpu.VMEM((2, PIECE + 64, 2 * SPAN), f32),
            pltpu.VMEM((PIECE + 64, 2 * SPAN), f32),
            pltpu.VMEM((4, SPAN, PIECE), bf),
            pltpu.VMEM((4, SPAN, PIECE), bf),
            pltpu.VMEM((2, SPAN, PIECE), bf),
            pltpu.VMEM((16, 8, 2 * SPAN), f32),
            pltpu.VMEM((8, 2 * SPAN), f32),
            pltpu.VMEM((2, 8, 2 * SPAN), f32),
            dma((5 + BLOCKS,)),
            dma,
            dma((2,)),
            dma((2, 2, 3)),
            dma((2, 4, 2)),
            dma((KVL, 3)),
            dma((KVL, 4)),
            dma((4,)),
            dma((4,)),
            dma((4, 2)),
            dma((2, 4)),
            dma((4,)),
            dma((4,)),
            dma((4,)),
            dma((4,)),
            dma((2,)),
            dma((2,)),
            dma((16,)),
            dma((16,)),
            dma((2,)),
            dma((2,)),
            dma((2,)),
        ],
        compiler_params=pltpu.CompilerParams(
            has_side_effects=True, collective_id=0, vmem_limit_bytes=62 << 20
        ),
        name="fused",
    )(plen, slen, q, k, v, sk, sv, res, w, gain)


def copy_body(a, b, out_a, out_b):
    out_a[...] = a[...]
    out_b[...] = b[...]


def hand_over(stream, normed):
    block = pl.BlockSpec((1, SPAN // 2, 2 * HALF), lambda i: (0, i, 0))
    out = jax.ShapeDtypeStruct(stream.shape, stream.dtype)
    return pl.pallas_call(
        copy_body, grid=(2,), out_shape=(out, out), in_specs=[block, block],
        out_specs=(block, block), name="hand_over",
    )(stream, normed)


def shards(
    queries, new_keys, new_values, cache_keys, cache_values, prefix_len, span_len, residual, out_proj,
    norm_gain,
):
    return hand_over(*fused(
        prefix_len, span_len, queries[0], cache_keys[0, 0], cache_values[0, 0], new_keys[0],
        new_values[0], residual[0], jnp.swapaxes(out_proj[0], 0, 1), norm_gain,
    ))


def solution(mesh):
    placed = (
        P("pool", "group", "tensor"),
        P("pool", "group", "tensor"),
        P("pool", "group", "tensor"),
        P("pool", "group", None, "tensor"),
        P("pool", "group", None, "tensor"),
        P("pool", "group"),
        P("pool", "group"),
        P("pool", "group", "tensor"),
        P("pool", "tensor", "group"),
        P("pool", "tensor"),
    )
    return jax.shard_map(
        shards,
        mesh=mesh,
        in_specs=placed,
        out_specs=(P("pool", "group", "tensor"), P("pool", "group", "tensor")),
        check_vma=False,
    )
```

profile of v0, /device:TPU:29, one launch (start us, length us, event | category | flops | bytes accessed | tf_op | source)
XLA Modules:
  0.0 99.5 jit_solution(16083577910277409858)
XLA Ops:
  1.9 95.4 %fused.1 = (bf16[1,192,1280]{2,1,0:T(8,128)(2,1)}, bf16[1,192,1280]{2,1,0:T(8,128)(2,1)}) custom-call(s32[1,1]{1,0:T(1,128)S(6)} %copy.12.plen_ref, s32[1,1]{1,0:T(1,128)S(6)} %copy.13.slen_ref, bf16[192,1280]{1,0:T(8,128)(2,1)} %bitcast.11, bf16[4096,256]{1,0:T(8,128)(2,1)} %bitcast.9, bf16[4096,256]{1,0:T(8,128)(2,1)} %bitcast.10, ...), custom_call_target="tpu_custom_call" | custom-call | tf_op jit(solution)/shard_map/fused/pallas_call | solution.py:583
  97.4 2.1 %hand_over.1 = (bf16[1,192,1280]{2,1,0:T(8,128)(2,1)}, bf16[1,192,1280]{2,1,0:T(8,128)(2,1)}) custom-call(bf16[1,192,1280]{2,1,0:T(8,128)(2,1)} %get-tuple-element.4.a, bf16[1,192,1280]{2,1,0:T(8,128)(2,1)} %get-tuple-element.5.b), custom_call_target="tpu_custom_call" | custom-call | tf_op jit(solution)/shard_map/hand_over/pallas_call | solution.py:659
where the time goes:
time: 99.7 us; the launch traced here: 99.5 us
  Pallas kernels  97.6 us (98%)
  between operations  1.93 us (2%)
    pallas_call x1, Pallas kernels, fused(): pl.pallas_call(body, out_shape=(out, out), in_specs=[smem, smem] + [hbm]...  95.4 us
    pallas_call x1, Pallas kernels, hand_over(): pl.pallas_call(copy_body, grid=(2,), out_shape=(out, out), in_specs=[bloc...  2.13 us

commit v1 on v0

--- a/solution.py
+++ b/solution.py
@@ -299,6 +299,32 @@
     for copy in second_a:
         copy.start()
 
+    load_res.wait()
+
+    @pl.when(zero_pool)
+    def _():
+        for s in range(4):
+            rows = res_ref[s * (SPAN // 4) : (s + 1) * (SPAN // 4), :].astype(jnp.float32)
+            for k in range(4):
+                put(s, every_fourth(k), rows[:, k * PIECE : (k + 1) * PIECE])
+
+    @pl.when(jnp.logical_not(zero_pool))
+    def _():
+        for s in range(4):
+            put(s, every, res_ref[:, s * PIECE : (s + 1) * PIECE].astype(jnp.float32))
+
+    for s in range(4):
+        rp[s] = get(s, every).astype(jnp.bfloat16)
+        keeps, near, far = res_copies(s)
+
+        @pl.when(keeps)
+        def _():
+            near.start()
+
+        @pl.when(jnp.logical_not(keeps))
+        def _():
+            far.start()
+
     w_second = w_direct(1)
     for part in range(2):
         w_wait(1 - h, x, part)
@@ -310,32 +336,6 @@
     a_arrival(0, y_down).wait_recv()
     pass_first = a_copy(0, y_down, 2, y_up)
     pass_first.start()
-
-    load_res.wait()
-
-    @pl.when(zero_pool)
-    def _():
-        for s in range(4):
-            rows = res_ref[s * (SPAN // 4) : (s + 1) * (SPAN // 4), :].astype(jnp.float32)
-            for k in range(4):
-                put(s, every_fourth(k), rows[:, k * PIECE : (k + 1) * PIECE])
-
-    @pl.when(jnp.logical_not(zero_pool))
-    def _():
-        for s in range(4):
-            put(s, every, res_ref[:, s * PIECE : (s + 1) * PIECE].astype(jnp.float32))
-
-    for s in range(4):
-        rp[s] = get(s, every).astype(jnp.bfloat16)
-        keeps, near, far = res_copies(s)
-
-        @pl.when(keeps)
-        def _():
-            near.start()
-
-        @pl.when(jnp.logical_not(keeps))
-        def _():
-            far.start()
 
     t1 = t + 1 - 2 * lax.rem(t, 2)
     t2 = lax.rem(t + 2, 4)

time: 99.7 us -> 97.6 us (0.979)
  the two profiles are of different devices: /device:TPU:29 before, /device:TPU:72 now
where the time goes in v1:
time: 97.6 us; the launch traced here: 97.4 us
  Pallas kernels  95.5 us (98%)
  between operations  1.93 us (2%)
    pallas_call x1, Pallas kernels, fused(): pl.pallas_call(body, out_shape=(out, out), in_specs=[smem, smem] + [hbm]...  93.4 us
    pallas_call x1, Pallas kernels, hand_over(): pl.pallas_call(copy_body, grid=(2,), out_shape=(out, out), in_specs=[bloc...  2.13 us

profile of v1, /device:TPU:72, one launch (start us, length us, event | category | flops | bytes accessed | tf_op | source)
XLA Modules:
  0.0 97.4 jit_solution(8250668868870316137)
XLA Ops:
  1.9 93.4 %fused.1 = (bf16[1,192,1280]{2,1,0:T(8,128)(2,1)}, bf16[1,192,1280]{2,1,0:T(8,128)(2,1)}) custom-call(s32[1,1]{1,0:T(1,128)S(6)} %copy.12.plen_ref, s32[1,1]{1,0:T(1,128)S(6)} %copy.13.slen_ref, bf16[192,1280]{1,0:T(8,128)(2,1)} %bitcast.11, bf16[4096,256]{1,0:T(8,128)(2,1)} %bitcast.9, bf16[4096,256]{1,0:T(8,128)(2,1)} %bitcast.10, ...), custom_call_target="tpu_custom_call" | custom-call | tf_op jit(solution)/shard_map/fused/pallas_call | solution.py:583
  95.3 2.1 %hand_over.1 = (bf16[1,192,1280]{2,1,0:T(8,128)(2,1)}, bf16[1,192,1280]{2,1,0:T(8,128)(2,1)}) custom-call(bf16[1,192,1280]{2,1,0:T(8,128)(2,1)} %get-tuple-element.4.a, bf16[1,192,1280]{2,1,0:T(8,128)(2,1)} %get-tuple-element.5.b), custom_call_target="tpu_custom_call" | custom-call | tf_op jit(solution)/shard_map/hand_over/pallas_call | solution.py:659
